TPU v7x, 256 devices: a whole 4x4x8 slice. The times are simulated.
256 devices in a mesh: stretch: 4 (over z_hi), space: 64 (over x, y, z_lo, core).
Axes of the slice: x: 4, y: 4, z: 8 (z_hi: 4, z_lo: 2; z = z_hi * 2 + z_lo), core: 2. Of those that a mesh axis runs over, the one named last changes fastest.
Arguments:
- queries: bfloat16 [4, 1024, 3072], P('stretch', 'space'), may hold values from -8 to 8
- stretch_keys: bfloat16 [4, 1024, 3072], P('stretch', 'space'), may hold values from -4 to 4
- stretch_values: bfloat16 [4, 1024, 3072], P('stretch', 'space'), may hold values from -6 to 6
- cache_keys: bfloat16 [32, 1024, 3072], P('stretch', 'space'), may hold values from -4 to 4
- cache_values: bfloat16 [32, 1024, 3072], P('stretch', 'space'), may hold values from -6 to 6
- block_list: int32 [4, 16], replicated, may hold values from 0 to 31, as said below
- list_len: int32 [4], replicated, may hold values from 4 to 16
- tok_count: int32 [4], replicated, may hold values from 512 to 1024, as said below
- noise_levels: int32 [4], replicated, may hold values from 0 to 47
- gate_table: float32 [48, 3072], replicated, may hold values from 0.1 to 1.9
Outputs:
- shifted: bfloat16 [4, 1024, 3072], P('stretch', 'space')
Inputs may be any that keep to these rules, and one draw needn't show every extreme that they name: `block_list`: stretch c's list names list_len[c] distinct blocks; the owner of block b is b // 8; at most 4 of one list's blocks have one owner, and every list has exactly 4 from some owner; in every draw one stretch's list is full, with 4 blocks from every owner, and another stretch's list holds exactly 4 blocks; entries from list_len[c] on are 0. `tok_count`: some stretch has all 1024 slots valid in every draw.
All inputs are finite; a program needn't handle non-finite values.
Results may differ from a plain program's by a relative error of at most 0.025.
Values may be sent and summed in bfloat16 or wider, within the bound.
A program may use at most 128 MiB of HBM per device.

v0:
```python
import functools
import math

import jax
import jax.numpy as jnp
from jax import lax
from jax.experimental import pallas as pl
from jax.experimental.pallas import tpu as pltpu
from jax.sharding import Mesh
from jax.sharding import PartitionSpec as P

HEAD_DIM = 128
LOCAL_HEADS = 3
COLS = LOCAL_HEADS * HEAD_DIM
PER_SRC = 4
MEMBERS = 8
ROWS = 16
CLEAN = 8
LIST = 16
STRETCHES = 4
KEYS = 256
QUERIES = 256
MASKED = -1e30
UNUSED = 1e30
SCALE = 1.4426950408889634 / math.sqrt(HEAD_DIM)
AXES = ("zh", "x", "yh", "yl", "zl", "core")
GROUP = [(dx, dl) for dx in (2, 1, 3, 0) for dl in (1, 0) if (dx, dl) != (0, 0)]
PLANE = [(dx, dh, dl) for dx in (2, 1, 3, 0) for dh in (1, 0) for dl in (1, 0) if (dx, dh, dl) != (0, 0, 0)]


class Place:
    def __init__(self):
        for name in AXES:
            setattr(self, name, lax.axis_index(name))
        self.z = self.zh * 2 + self.zl
        self.member = self.x * 2 + self.yl

    def peer(self, dx, dl):
        px, pyl = (self.x + dx) % 4, (self.yl + dl) % 2
        return {"x": px, "yl": pyl}, px * 2 + pyl

    def in_plane(self, dx, dh, dl):
        target, member = self.peer(dx, dl)
        return dict(target, yh=(self.yh + dh) % 2), member

    def to_z(self, step):
        other = (self.z + step + 8) % 8
        return {"zh": other // 2, "zl": other % 2}

    def to_y(self):
        return {"yh": 1 - self.yh}

    def to_core(self):
        return {"core": 1 - self.core}


def greet(targets):
    barrier = pltpu.get_barrier_semaphore()
    for target in targets:
        pl.semaphore_signal(barrier, inc=1, device_id=target, device_id_type=pl.DeviceIdType.MESH)
    pl.semaphore_wait(barrier, len(targets))


def remote(src, dst, send, recv, target):
    return pltpu.make_async_remote_copy(
        src_ref=src, dst_ref=dst, send_sem=send, recv_sem=recv, device_id=target, device_id_type=pl.DeviceIdType.MESH
    )


def drain(ref, sem):
    pltpu.make_async_copy(ref, ref, sem).wait()


def aligned(start, size):
    return pl.ds(pl.multiple_of(start, size), size)


def dot_rows(a, b):
    return lax.dot_general(a, b, (((1,), (1,)), ((), ())), preferred_element_type=jnp.float32)


def merge(parts):
    top = functools.reduce(jnp.maximum, [t for _, t, _ in parts])
    factors = [jnp.exp2(t - top) for _, t, _ in parts]
    total = functools.reduce(jnp.add, [f * n for f, (_, _, n) in zip(factors, parts)])
    sums = functools.reduce(jnp.add, [s.astype(jnp.float32) * f for f, (s, _, _) in zip(factors, parts)])
    return sums, top, total


def read_stats(ref):
    tile = ref[...]
    return [(tile[i : i + 1], tile[2 + i : 3 + i]) for i in (0, 1)]


def write_stats(ref, half, top, total):
    ref[half : half + 1, :] = top
    ref[2 + half : 3 + half, :] = total


def kernel(
    block_list, list_len, tok_count, noise_levels, q, sk, sv, ck, cv, gate_table, out,
    keys0, keys1, keys2, values0, values1, values2, kept, turned, scores0, scores1, staged, stage_sem, queries, own_bias, picked,
    sums, stats, held, held_stats, got, got_stats, y_held, y_held_stats, y_got, y_got_stats, gates, ready,
    kv_send, kv_recv, core_send, core_recv, q_send, q_recv, ring_send, ring_recv,
    p_send, p_recv, t_send, t_recv, y_send, y_recv, out_send, out_recv, gate_sem,
):
    at = Place()
    keys, values = (keys0, keys1, keys2), (values0, values1, values2)
    staging = [
        pltpu.make_async_copy(ck, staged.at[0, pl.ds(0, CLEAN)], stage_sem.at[0]),
        pltpu.make_async_copy(cv, staged.at[1, pl.ds(0, CLEAN)], stage_sem.at[1]),
        pltpu.make_async_copy(sk, staged.at[0, pl.ds(CLEAN, 1)], stage_sem.at[2]),
        pltpu.make_async_copy(sv, staged.at[1, pl.ds(CLEAN, 1)], stage_sem.at[3]),
    ]
    for copy in staging:
        copy.start()
    greet([at.in_plane(*off)[0] for off in PLANE] + [at.to_z(1), at.to_z(-1), at.to_core()])

    q_rows = aligned(at.yh * 128 + at.member * ROWS, ROWS)
    q_dst = queries.at[at.z, q_rows, :]
    for off in PLANE:
        target, member = at.in_plane(*off)
        remote(q.at[0, :, aligned(member * COLS, COLS)], q_dst, q_send, q_recv, target).start()
    pltpu.make_async_copy(q.at[0, :, aligned(at.member * COLS, COLS)], q_dst, q_recv).start()

    slot = aligned((at.core * MEMBERS + at.member) * ROWS, ROWS)
    my_half = aligned(at.core * 128, 128)

    def send_keys(h):
        for part, ref in enumerate((keys[h], values[h])):
            dst = ref.at[:, slot, :]
            for off in GROUP:
                target, member = at.peer(*off)
                cols = aligned(member * COLS + h * HEAD_DIM, HEAD_DIM)
                remote(staged.at[part, :, :, cols], dst, kv_send.at[h, part], kv_recv.at[h, part], target).start()
            cols = aligned(at.member * COLS + h * HEAD_DIM, HEAD_DIM)
            pltpu.make_async_copy(staged.at[part, :, :, cols], dst, kv_recv.at[h, part]).start()

    def share_copy(h, part):
        ref = (keys[h], values[h])[part].at[:, my_half, :]
        return remote(ref, ref, core_send.at[h, part], core_recv.at[h, part], at.to_core())

    def share_keys(h):
        for part, ref in enumerate((keys[h], values[h])):
            drain(ref.at[:, my_half, :], kv_recv.at[h, part])
            share_copy(h, part).start()

    def take_keys(h):
        for part in (0, 1):
            share_copy(h, part).wait_recv()

        def turn(block, carry):
            kept[h, block] = keys[h][block]
            turned[h, block] = values[h][block].T
            return carry

        lax.fori_loop(0, CLEAN + 1, turn, 0)

    def ring_copy(h, step, side):
        plane = (at.z - step + 8) % 8 if side == 0 else (at.z + step) % 8
        rows = pl.ds(side * 128, 128) if step == 3 else pl.ds(0, QUERIES)
        piece = queries.at[plane, rows, pl.ds(h * HEAD_DIM, HEAD_DIM)]
        return remote(
            piece, piece, ring_send.at[h, step, side], ring_recv.at[h, step, side], at.to_z(1 if side == 0 else -1)
        )

    def ring_step(h, step):
        for side in (0, 1):
            if step > 0:
                ring_copy(h, step - 1, side).wait_recv()
            ring_copy(h, step, side).start()

    def ring_end(h):
        for side in (0, 1):
            ring_copy(h, 3, side).wait_recv()

    def dest_of(step, side):
        return (at.z + 4 + step) % 8 if side == 0 else (at.z + 4 - step) % 8

    def sum_copies(h, step, side):
        target = at.to_z(-1 if side == 0 else 1)
        dest = dest_of(step, side)
        if step == 0:
            lanes = pl.ds(side * 128, 128)
            src, src_stats = sums.at[h, dest, :, lanes], stats.at[h, dest]
        else:
            lanes = pl.ds(0, QUERIES)
            src, src_stats = held.at[h, step - 1, side], held_stats.at[h, step - 1, side]
        return [
            remote(src, got.at[h, step, side, :, lanes], p_send.at[h, step, side], p_recv.at[h, step, side], target),
            remote(src_stats, got_stats.at[h, step, side], t_send.at[h, step, side], t_recv.at[h, step, side], target),
        ]

    def sum_step(h, step):
        for side in (0, 1):
            if step > 0:
                for copy in sum_copies(h, step - 1, side):
                    copy.wait_recv()
                dest = dest_of(step, side)
                mine, theirs = read_stats(stats.at[h, dest]), read_stats(got_stats.at[h, step - 1, side])
                to_stats = held_stats.at[h, step - 1, side]
                for half in (0, 1):
                    lanes = slice(half * 128, half * 128 + 128)
                    if step == 1 and half != side:
                        held[h, 0, side, :, lanes] = sums[h, dest, :, lanes]
                        write_stats(to_stats, half, *mine[half])
                        continue
                    merged, top, total = merge(
                        [(sums[h, dest, :, lanes], *mine[half]), (got[h, step - 1, side, :, lanes], *theirs[half])]
                    )
                    held[h, step - 1, side, :, lanes] = merged.astype(jnp.bfloat16)
                    write_stats(to_stats, half, top, total)
            for copy in sum_copies(h, step, side):
                copy.start()

    def gathered(h, half):
        lanes = pl.ds(half * 128, 128)
        sources = [
            (sums.at[h, at.z], stats.at[h, at.z]),
            (got.at[h, 3, 0], got_stats.at[h, 3, 0]),
            (got.at[h, 3, 1], got_stats.at[h, 3, 1]),
        ]
        return [(ref[:, lanes], *read_stats(stat)[half]) for ref, stat in sources]

    def y_copies(h):
        return [
            remote(y_held.at[h], y_got.at[h], y_send.at[h, 0], y_recv.at[h, 0], at.to_y()),
            remote(y_held_stats.at[h], y_got_stats.at[h], y_send.at[h, 1], y_recv.at[h, 1], at.to_y()),
        ]

    def sum_end(h):
        for side in (0, 1):
            for copy in sum_copies(h, 3, side):
                copy.wait_recv()
        for half in (0, 1):

            @pl.when(at.yh != half)
            def _():
                merged, top, total = merge(gathered(h, half))
                y_held[h] = merged.astype(jnp.bfloat16)
                write_stats(y_held_stats.at[h], 0, top, total)

        for copy in y_copies(h):
            copy.start()

    stretch_out = (at.zh + 3) % 4

    def finish(h):
        for copy in y_copies(h):
            copy.wait_recv()
        r = lax.broadcasted_iota(jnp.int32, (128, HEAD_DIM), 0)
        position = (r // 32) * 256 + at.yh * 128 + ((r // 16) % 2) * 64 + at.zl * 32 + at.core * 16 + r % 16
        keep = position < tok_count[stretch_out]
        cols = pl.ds(h * HEAD_DIM, HEAD_DIM)
        gate_row = gates[pl.ds(noise_levels[stretch_out], 1), :][:, h * HEAD_DIM : (h + 1) * HEAD_DIM]
        for half in (0, 1):

            @pl.when(at.yh == half)
            def _():
                merged, top, total = merge(gathered(h, half) + [(y_got[h], *read_stats(y_got_stats.at[h])[0])])
                attended = merged / total
                mean_sq = jnp.mean(attended * attended, axis=0, keepdims=True)
                normed = (attended * lax.rsqrt(mean_sq + 1e-6)).T
                ready[:, cols] = jnp.where(keep, normed * gate_row, 0.0).astype(jnp.bfloat16)

        dst = out.at[0, :, aligned(at.member * COLS + h * HEAD_DIM, HEAD_DIM)]
        for off in GROUP:
            target, member = at.peer(*off)
            remote(ready.at[aligned(member * ROWS, ROWS), cols], dst, out_send.at[h], out_recv.at[h], target).start()
        pltpu.make_async_copy(ready.at[aligned(at.member * ROWS, ROWS), cols], dst, out_recv.at[h]).start()

    def query_rows(h, dest):
        plane = (dest + 6) % 8
        return plane // 2, queries[plane, :, h * HEAD_DIM : (h + 1) * HEAD_DIM]

    def fold(x, op):
        return op(x.reshape(-1, 8, QUERIES), axis=0)

    def stage(cur, cur_scores, top, nxt, nxt_scores):
        if cur is not None:
            h, dest = cur
            stretch = (dest + 6) % 8 // 2
            shift = top * SCALE
            total8 = jnp.zeros((8, QUERIES), jnp.float32)
            product = None
        if nxt is not None:
            next_h = nxt[0]
            next_stretch, q_head = query_rows(*nxt)
            top8 = jnp.full((8, QUERIES), MASKED, jnp.float32)
        for e in range(PER_SRC):
            rows = slice(e * KEYS, (e + 1) * KEYS)
            if nxt is not None:
                scores = dot_rows(kept[next_h, picked[next_stretch, e]], q_head)
                nxt_scores[rows, :] = scores
                live = e < picked[next_stretch, PER_SRC]
                top8 = jnp.maximum(top8, jnp.where(live, fold(scores, jnp.max), MASKED))
            if cur is not None:
                live = e < picked[stretch, PER_SRC]
                weights = jnp.exp2(cur_scores[rows, :] * SCALE - jnp.where(live, shift, UNUSED))
                total8 = total8 + fold(weights, jnp.sum)
                part = jnp.dot(
                    turned[h, picked[stretch, e]], weights.astype(jnp.bfloat16), preferred_element_type=jnp.float32
                )
                product = part if product is None else product + part
        if cur is not None:
            sums[h, dest] = product.astype(jnp.bfloat16)
            total = jnp.sum(total8, axis=0, keepdims=True)
            for half in (0, 1):
                lanes = slice(half * 128, half * 128 + 128)
                write_stats(stats.at[h, dest], half, shift[:, lanes], total[:, lanes])
        return None if nxt is None else jnp.max(top8, axis=0, keepdims=True)

    def add_own(h, dest):
        @pl.when((dest + 6) % 8 // 2 == at.zh)
        def _():
            _, q_head = query_rows(h, dest)
            bias = own_bias[...]
            scores = dot_rows(kept[h, CLEAN], q_head) + jnp.concatenate([bias, bias], axis=1)
            shift = jnp.max(scores, axis=0, keepdims=True) * SCALE
            weights = jnp.exp2(scores * SCALE - shift)
            total = jnp.sum(weights, axis=0, keepdims=True)
            product = jnp.dot(turned[h, CLEAN], weights.astype(jnp.bfloat16), preferred_element_type=jnp.float32)
            before = read_stats(stats.at[h, dest])
            for half in (0, 1):
                lanes = slice(half * 128, half * 128 + 128)
                merged, top, total_both = merge(
                    [(sums[h, dest, :, lanes], *before[half]), (product[:, lanes], shift[:, lanes], total[:, lanes])]
                )
                sums[h, dest, :, lanes] = merged.astype(jnp.bfloat16)
                write_stats(stats.at[h, dest], half, top, total_both)

    gate_copy = pltpu.make_async_copy(gate_table.at[:, aligned(at.member * COLS, COLS)], gates, gate_sem)

    for copy in staging:
        copy.wait()
    for h in range(LOCAL_HEADS):
        send_keys(h)
    gate_copy.start()
    for stretch in range(STRETCHES):
        count = jnp.int32(0)
        chosen = [jnp.int32(0)] * PER_SRC
        for entry in range(LIST):
            block = block_list[stretch, entry]
            hit = jnp.logical_and(block // CLEAN == at.zh, entry < list_len[stretch])
            for e in range(PER_SRC):
                chosen[e] = jnp.where(jnp.logical_and(hit, count == e), block % CLEAN, chosen[e])
            count = count + jnp.where(hit, 1, 0)
        for e in range(PER_SRC):
            picked[stretch, e] = chosen[e]
        picked[stretch, PER_SRC] = count
    j = lax.broadcasted_iota(jnp.int32, (KEYS, 128), 0)
    position = ((j // 32) % 4) * 256 + at.yh * 128 + ((j // 16) % 2) * 64 + at.zl * 32 + (j // 128) * 16 + j % 16
    own_bias[...] = jnp.where(position < tok_count[at.zh], 0.0, MASKED)
    drain(queries.at[at.z], q_recv)
    for h in range(LOCAL_HEADS):
        ring_step(h, 0)
    share_keys(0)
    for h in range(LOCAL_HEADS):
        ring_step(h, 1)
    take_keys(0)
    for h in range(LOCAL_HEADS):
        ring_step(h, 2)
    share_keys(1)
    gate_copy.wait()
    take_keys(1)

    def dest_at(u):
        away = 4 - (u + 1) // 2
        return jnp.where(u % 2 == 1, at.z + away, at.z + 8 - away) % 8

    def first_heads(u, top):
        pl.when(u == 1)(lambda: ring_step(0, 3))
        pl.when(u == 1)(lambda: ring_step(1, 3))
        pl.when(u == 2)(lambda: ring_step(2, 3))
        pl.when(u == 3)(lambda: ring_end(0))
        pl.when(u == 3)(lambda: ring_end(1))
        pl.when(u == 5)(lambda: share_keys(2))
        dest, later = dest_at(u), dest_at(jnp.minimum(u + 1, 7))
        top = stage((0, dest), scores0, top, (1, dest), scores1)
        add_own(0, dest)
        top = stage((1, dest), scores1, top, (0, later), scores0)
        add_own(1, dest)
        for h in (0, 1):
            pl.when(u == 0)(functools.partial(sum_step, h, 0))
            pl.when(u == 2)(functools.partial(sum_step, h, 1))
            pl.when(u == 5)(functools.partial(sum_step, h, 2))
        return top

    top = stage(None, None, None, (0, dest_at(0)), scores0)
    lax.fori_loop(0, 8, first_heads, top)
    take_keys(2)
    ring_end(2)

    def last_head(i, top):
        even, odd, later = dest_at(2 * i), dest_at(2 * i + 1), dest_at(jnp.minimum(2 * i + 2, 7))
        top = stage((2, even), scores0, top, (2, odd), scores1)
        add_own(2, even)
        pl.when(i == 0)(lambda: sum_step(2, 0))
        top = stage((2, odd), scores1, top, (2, later), scores0)
        add_own(2, odd)
        for h in (0, 1):
            pl.when(i == 0)(functools.partial(sum_step, h, 3))
        return top

    top = stage(None, None, None, (2, dest_at(0)), scores0)
    lax.fori_loop(0, 4, last_head, top)
    sum_step(2, 1)
    sum_end(0)
    sum_end(1)
    sum_step(2, 2)
    finish(0)
    finish(1)
    sum_step(2, 3)
    sum_end(2)
    finish(2)

    drain(queries.at[0, pl.ds(0, 15 * ROWS), :], q_send)
    for h in range(LOCAL_HEADS):
        for part, ref in enumerate((keys[h], values[h])):
            drain(ref.at[:, pl.ds(0, 7 * ROWS), :], kv_send.at[h, part])
            share_copy(h, part).wait_send()
        for side in (0, 1):
            for step in range(4):
                ring_copy(h, step, side).wait_send()
                for copy in sum_copies(h, step, side):
                    copy.wait_send()
        for copy in y_copies(h):
            copy.wait_send()
        drain(ready.at[pl.ds(0, 7 * ROWS), pl.ds(0, HEAD_DIM)], out_send.at[h])
        drain(out.at[0, :, pl.ds(0, MEMBERS * HEAD_DIM)], out_recv.at[h])


def shards(q, sk, sv, ck, cv, block_list, list_len, tok_count, noise_levels, gate_table):
    smem = pl.BlockSpec(memory_space=pltpu.SMEM)
    hbm = pl.BlockSpec(memory_space=pltpu.HBM)
    dma = pltpu.SemaphoreType.DMA
    bf, f32 = jnp.bfloat16, jnp.float32
    heads = LOCAL_HEADS
    return pl.pallas_call(
        kernel,
        out_shape=jax.ShapeDtypeStruct((1, ROWS, MEMBERS * COLS), bf),
        in_specs=[smem] * 4 + [hbm] * 6,
        out_specs=hbm,
        scratch_shapes=[pltpu.VMEM((CLEAN + 1, KEYS, HEAD_DIM), bf)] * 6
        + [
            pltpu.VMEM((heads, CLEAN + 1, KEYS, HEAD_DIM), bf),
            pltpu.VMEM((heads, CLEAN + 1, HEAD_DIM, KEYS), bf),
            pltpu.VMEM((PER_SRC * KEYS, QUERIES), f32),
            pltpu.VMEM((PER_SRC * KEYS, QUERIES), f32),
            pltpu.VMEM((2, CLEAN + 1, ROWS, MEMBERS * COLS), bf),
            dma((4,)),
            pltpu.VMEM((8, QUERIES, COLS), bf),
            pltpu.VMEM((KEYS, 128), f32),
            pltpu.SMEM((STRETCHES, PER_SRC + 1), jnp.int32),
            pltpu.VMEM((heads, 8, HEAD_DIM, QUERIES), bf),
            pltpu.VMEM((heads, 8, 8, 128), f32),
            pltpu.VMEM((heads, 3, 2, HEAD_DIM, QUERIES), bf),
            pltpu.VMEM((heads, 3, 2, 8, 128), f32),
            pltpu.VMEM((heads, 4, 2, HEAD_DIM, QUERIES), bf),
            pltpu.VMEM((heads, 4, 2, 8, 128), f32),
            pltpu.VMEM((heads, HEAD_DIM, 128), bf),
            pltpu.VMEM((heads, 8, 128), f32),
            pltpu.VMEM((heads, HEAD_DIM, 128), bf),
            pltpu.VMEM((heads, 8, 128), f32),
            pltpu.VMEM((48, COLS), f32),
            pltpu.VMEM((128, COLS), bf),
            dma((heads, 2)), dma((heads, 2)), dma((heads, 2)), dma((heads, 2)), dma, dma,
            dma((heads, 4, 2)), dma((heads, 4, 2)), dma((heads, 4, 2)), dma((heads, 4, 2)),
            dma((heads, 4, 2)), dma((heads, 4, 2)), dma((heads, 2)), dma((heads, 2)), dma((heads,)), dma((heads,)), dma,
        ],
        compiler_params=pltpu.CompilerParams(
            collective_id=0, has_side_effects=True, vmem_limit_bytes=58 * 1024 * 1024
        ),
    )(block_list, list_len, tok_count, noise_levels, q, sk, sv, ck, cv, gate_table)


def solution(mesh):
    fine = Mesh(mesh.devices.reshape(4, 4, 2, 2, 2, 2), AXES)
    split = P("zh", ("x", "yh", "yl", "zl", "core"), None)
    return jax.shard_map(
        shards, mesh=fine, in_specs=(split,) * 5 + (P(),) * 5, out_specs=split, check_vma=False
    )
```

profile of v0, /device:TPU:8, one launch (start us, length us, event | category | flops | bytes accessed | tf_op | source)
XLA Modules:
  0.0 70.6 jit_solution(9554778929788281310)
XLA Ops:
  0.0 69.1 %shard_map.100 = bf16[1,16,3072]{2,1,0:T(8,128)(2,1)} custom-call(s32[4,16]{1,0:T(4,128)} %block_list.1, s32[4]{0:T(128)} %list_len.1, s32[4]{0:T(128)} %tok_count.1, s32[4]{0:T(128)} %noise_levels.1, bf16[1,16,3072]{2,1,0:T(8,128)(2,1)} %q.1, bf16[1,16,3072]{2,1,0:T(8,128)(2,1)} %sk.1, bf16[1,16,3072]{2,1,0:T(8,128)(2,1)} %sv.1, bf16[8,16,3072]{2,1,0:T(8,128)(2,1)} %ck.1, ...), custom_call_target="tpu_custom_call" | custom-call | tf_op jit(solution)/shard_map/pallas_call | solution.py:439
  69.1 1.5 %copy.12 = bf16[1,16,3072]{2,1,0:T(8,128)(2,1)} copy(bf16[1,16,3072]{2,1,0:T(8,128)(2,1)} %shard_map.100) | data formatting | bytes 196608
where the time goes:
time: 70.7 us; the launch traced here: 70.6 us
  Pallas kernels  69.1 us (98%)
  local copies, waits for them, and re-layouts  1.54 us (2%)
    pallas_call x1, Pallas kernels, shards(): pl.pallas_call(kernel, out_shape=jax.ShapeDtypeStruct((1, ROWS, MEMBERS *...  69.1 us
    unnamed x1, local copies, waits for them, and re-layouts  1.54 us

commit v1 on v0

--- a/solution.py
+++ b/solution.py
@@ -98,11 +98,11 @@
 
 
 def kernel(
-    block_list, list_len, tok_count, noise_levels, q, sk, sv, ck, cv, gate_table, out,
-    keys0, keys1, keys2, values0, values1, values2, kept, turned, scores0, scores1, staged, stage_sem, queries, own_bias, picked,
-    sums, stats, held, held_stats, got, got_stats, y_held, y_held_stats, y_got, y_got_stats, gates, ready,
+    block_list_hbm, list_len_hbm, tok_count_hbm, noise_levels_hbm, q, sk, sv, ck, cv, gate_table, out,
+    block_list, list_len, tok_count, noise_levels, scalar_sem, keys0, keys1, keys2, values0, values1, values2, kept, turned, scores0, scores1, staged, stage_sem, queries, own_bias, picked,
+    sums, stats, y_got, y_got_stats, joined, joined_stats, z_got, z_got_stats, gates, ready,
     kv_send, kv_recv, core_send, core_recv, q_send, q_recv, ring_send, ring_recv,
-    p_send, p_recv, t_send, t_recv, y_send, y_recv, out_send, out_recv, gate_sem,
+    y_send, y_recv, z_send, z_recv, out_send, out_recv, gate_sem,
 ):
     at = Place()
     keys, values = (keys0, keys1, keys2), (values0, values1, values2)
@@ -112,9 +112,18 @@
         pltpu.make_async_copy(sk, staged.at[0, pl.ds(CLEAN, 1)], stage_sem.at[2]),
         pltpu.make_async_copy(sv, staged.at[1, pl.ds(CLEAN, 1)], stage_sem.at[3]),
     ]
-    for copy in staging:
+    scalars = [
+        pltpu.make_async_copy(src, dst, scalar_sem.at[n])
+        for n, (src, dst) in enumerate(
+            (
+                (block_list_hbm, block_list), (list_len_hbm, list_len), (tok_count_hbm, tok_count),
+                (noise_levels_hbm, noise_levels),
+            )
+        )
+    ]
+    for copy in staging + scalars:
         copy.start()
-    greet([at.in_plane(*off)[0] for off in PLANE] + [at.to_z(1), at.to_z(-1), at.to_core()])
+    greet([at.in_plane(*off)[0] for off in PLANE] + [*[at.to_z(k) for k in (1, -1, 2, -2)], at.to_core()])
 
     q_rows = aligned(at.yh * 128 + at.member * ROWS, ROWS)
     q_dst = queries.at[at.z, q_rows, :]
@@ -174,94 +183,100 @@
         for side in (0, 1):
             ring_copy(h, 3, side).wait_recv()
 
-    def dest_of(step, side):
-        return (at.z + 4 + step) % 8 if side == 0 else (at.z + 4 - step) % 8
-
-    def sum_copies(h, step, side):
-        target = at.to_z(-1 if side == 0 else 1)
-        dest = dest_of(step, side)
-        if step == 0:
-            lanes = pl.ds(side * 128, 128)
-            src, src_stats = sums.at[h, dest, :, lanes], stats.at[h, dest]
-        else:
-            lanes = pl.ds(0, QUERIES)
-            src, src_stats = held.at[h, step - 1, side], held_stats.at[h, step - 1, side]
+    my_lanes, other_lanes = aligned(at.yh * 128, 128), aligned((1 - at.yh) * 128, 128)
+
+    def y_copies(h, dest):
         return [
-            remote(src, got.at[h, step, side, :, lanes], p_send.at[h, step, side], p_recv.at[h, step, side], target),
-            remote(src_stats, got_stats.at[h, step, side], t_send.at[h, step, side], t_recv.at[h, step, side], target),
+            remote(
+                sums.at[h, dest, :, other_lanes], y_got.at[h, dest], y_send.at[h, dest, 0], y_recv.at[h, dest, 0], at.to_y()
+            ),
+            remote(stats.at[h, dest], y_got_stats.at[h, dest], y_send.at[h, dest, 1], y_recv.at[h, dest, 1], at.to_y()),
         ]
 
-    def sum_step(h, step):
+    def send_y(h, dest):
+        for copy in y_copies(h, dest):
+            copy.start()
+
+    def z_copies(h, dest, slot, step):
+        src, target = joined.at[h, dest], at.to_z(step)
+        return [
+            remote(src, z_got.at[h, slot], z_send.at[h, slot, 0], z_recv.at[h, slot, 0], target),
+            remote(
+                joined_stats.at[h, dest], z_got_stats.at[h, slot], z_send.at[h, slot, 1], z_recv.at[h, slot, 1], target
+            ),
+        ]
+
+    def z_start(h, dest, slot, step):
+        for copy in z_copies(h, dest, slot, step):
+            copy.start()
+
+    def z_part(h, slot):
+        drain(z_got.at[h, slot], z_recv.at[h, slot, 0])
+        drain(z_got_stats.at[h, slot], z_recv.at[h, slot, 1])
+        return (z_got[h, slot], *read_stats(z_got_stats.at[h, slot])[0])
+
+    def own_part(h, dest):
+        return (joined[h, dest], *read_stats(joined_stats.at[h, dest])[0])
+
+    def put_joined(h, dest, merged, top, total):
+        joined[h, dest] = merged.astype(jnp.bfloat16)
+        write_stats(joined_stats.at[h, dest], 0, top, total)
+
+    def middle(h):
         for side in (0, 1):
-            if step > 0:
-                for copy in sum_copies(h, step - 1, side):
-                    copy.wait_recv()
-                dest = dest_of(step, side)
-                mine, theirs = read_stats(stats.at[h, dest]), read_stats(got_stats.at[h, step - 1, side])
-                to_stats = held_stats.at[h, step - 1, side]
-                for half in (0, 1):
-                    lanes = slice(half * 128, half * 128 + 128)
-                    if step == 1 and half != side:
-                        held[h, 0, side, :, lanes] = sums[h, dest, :, lanes]
-                        write_stats(to_stats, half, *mine[half])
-                        continue
-                    merged, top, total = merge(
-                        [(sums[h, dest, :, lanes], *mine[half]), (got[h, step - 1, side, :, lanes], *theirs[half])]
-                    )
-                    held[h, step - 1, side, :, lanes] = merged.astype(jnp.bfloat16)
-                    write_stats(to_stats, half, top, total)
-            for copy in sum_copies(h, step, side):
-                copy.start()
-
-    def gathered(h, half):
-        lanes = pl.ds(half * 128, 128)
-        sources = [
-            (sums.at[h, at.z], stats.at[h, at.z]),
-            (got.at[h, 3, 0], got_stats.at[h, 3, 0]),
-            (got.at[h, 3, 1], got_stats.at[h, 3, 1]),
-        ]
-        return [(ref[:, lanes], *read_stats(stat)[half]) for ref, stat in sources]
-
-    def y_copies(h):
-        return [
-            remote(y_held.at[h], y_got.at[h], y_send.at[h, 0], y_recv.at[h, 0], at.to_y()),
-            remote(y_held_stats.at[h], y_got_stats.at[h], y_send.at[h, 1], y_recv.at[h, 1], at.to_y()),
-        ]
-
-    def sum_end(h):
-        for side in (0, 1):
-            for copy in sum_copies(h, 3, side):
-                copy.wait_recv()
-        for half in (0, 1):
-
-            @pl.when(at.yh != half)
+            dest = (at.z + (6, 2)[side]) % 8
+
+            @pl.when(at.z % 2 == side)
             def _():
-                merged, top, total = merge(gathered(h, half))
-                y_held[h] = merged.astype(jnp.bfloat16)
-                write_stats(y_held_stats.at[h], 0, top, total)
-
-        for copy in y_copies(h):
-            copy.start()
+                put_joined(h, dest, *merge([own_part(h, dest), z_part(h, 2 + side), z_part(h, 4 + side)]))
+
+            @pl.when(at.z % 2 != side)
+            def _():
+                put_joined(h, dest, *merge([own_part(h, dest), z_part(h, 2 + side)]))
+
+            z_start(h, dest, 6 + side, (-2, 2)[side])
+
+    def pick_half(ref):
+        tile = ref[...]
+        return [jnp.where(at.yh == 0, tile[i : i + 1], tile[i + 1 : i + 2]) for i in (0, 2)]
+
+    def join_y(h, dest):
+        for copy in y_copies(h, dest):
+            copy.wait_recv()
+        merged, top, total = merge(
+            [
+                (sums[h, dest, :, my_lanes], *pick_half(stats.at[h, dest])),
+                (y_got[h, dest], *pick_half(y_got_stats.at[h, dest])),
+            ]
+        )
+        put_joined(h, dest, merged, top, total)
+        away = (at.z - dest + 8) % 8
+        above = away < 4
+
+        @pl.when(away % 2 == 1)
+        def _():
+            slot = jnp.where(above, 0, 1) + jnp.where(jnp.logical_or(away == 3, away == 5), 2, 0)
+            z_start(h, dest, slot, jnp.where(above, -1, 1))
+
+        @pl.when(away == 4)
+        def _():
+            even = at.z % 2 == 0
+            z_start(h, dest, jnp.where(even, 4, 5), jnp.where(even, -2, 2))
 
     stretch_out = (at.zh + 3) % 4
 
     def finish(h):
-        for copy in y_copies(h):
-            copy.wait_recv()
+        parts = [own_part(h, at.z)] + [z_part(h, slot) for slot in (0, 1, 6, 7)]
         r = lax.broadcasted_iota(jnp.int32, (128, HEAD_DIM), 0)
         position = (r // 32) * 256 + at.yh * 128 + ((r // 16) % 2) * 64 + at.zl * 32 + at.core * 16 + r % 16
         keep = position < tok_count[stretch_out]
         cols = pl.ds(h * HEAD_DIM, HEAD_DIM)
         gate_row = gates[pl.ds(noise_levels[stretch_out], 1), :][:, h * HEAD_DIM : (h + 1) * HEAD_DIM]
-        for half in (0, 1):
-
-            @pl.when(at.yh == half)
-            def _():
-                merged, top, total = merge(gathered(h, half) + [(y_got[h], *read_stats(y_got_stats.at[h])[0])])
-                attended = merged / total
-                mean_sq = jnp.mean(attended * attended, axis=0, keepdims=True)
-                normed = (attended * lax.rsqrt(mean_sq + 1e-6)).T
-                ready[:, cols] = jnp.where(keep, normed * gate_row, 0.0).astype(jnp.bfloat16)
+        merged, top, total = merge(parts)
+        attended = merged / total
+        mean_sq = jnp.mean(attended * attended, axis=0, keepdims=True)
+        normed = (attended * lax.rsqrt(mean_sq + 1e-6)).T
+        ready[:, cols] = jnp.where(keep, normed * gate_row, 0.0).astype(jnp.bfloat16)
 
         dst = out.at[0, :, aligned(at.member * COLS + h * HEAD_DIM, HEAD_DIM)]
         for off in GROUP:
@@ -271,7 +286,7 @@
 
     def query_rows(h, dest):
         plane = (dest + 6) % 8
-        return plane // 2, queries[plane, :, h * HEAD_DIM : (h + 1) * HEAD_DIM]
+        return plane // 2, queries[plane, :, aligned(h * HEAD_DIM, HEAD_DIM)]
 
     def fold(x, op):
         return op(x.reshape(-1, 8, QUERIES), axis=0)
@@ -336,6 +351,8 @@
     for h in range(LOCAL_HEADS):
         send_keys(h)
     gate_copy.start()
+    for copy in scalars:
+        copy.wait()
     for stretch in range(STRETCHES):
         count = jnp.int32(0)
         chosen = [jnp.int32(0)] * PER_SRC
@@ -354,64 +371,59 @@
     drain(queries.at[at.z], q_recv)
     for h in range(LOCAL_HEADS):
         ring_step(h, 0)
-    share_keys(0)
     for h in range(LOCAL_HEADS):
         ring_step(h, 1)
+    share_keys(0)
+    gate_copy.wait()
     take_keys(0)
-    for h in range(LOCAL_HEADS):
-        ring_step(h, 2)
-    share_keys(1)
-    gate_copy.wait()
-    take_keys(1)
-
-    def dest_at(u):
-        away = 4 - (u + 1) // 2
-        return jnp.where(u % 2 == 1, at.z + away, at.z + 8 - away) % 8
-
-    def first_heads(u, top):
-        pl.when(u == 1)(lambda: ring_step(0, 3))
-        pl.when(u == 1)(lambda: ring_step(1, 3))
-        pl.when(u == 2)(lambda: ring_step(2, 3))
-        pl.when(u == 3)(lambda: ring_end(0))
-        pl.when(u == 3)(lambda: ring_end(1))
-        pl.when(u == 5)(lambda: share_keys(2))
-        dest, later = dest_at(u), dest_at(jnp.minimum(u + 1, 7))
-        top = stage((0, dest), scores0, top, (1, dest), scores1)
-        add_own(0, dest)
-        top = stage((1, dest), scores1, top, (0, later), scores0)
-        add_own(1, dest)
+
+    def unit_at(p):
+        near, far = p < 10, p < 16
+        h = jnp.where(near, p // 5, jnp.where(far, p % 2, 2))
+        u = jnp.where(near, p % 5, jnp.where(far, p // 2, p - 16))
+        near_first = 2 + jnp.where(u % 2 == 1, (u + 1) // 2, 8 - u // 2)
+        far_first = jnp.where(u % 2 == 1, 3 - u // 2, 4 + u // 2)
+        return h, (at.z + jnp.where(far, near_first, far_first)) % 8
+
+    def pair(i, top):
+        for h in range(LOCAL_HEADS):
+            pl.when(i == 1)(functools.partial(ring_step, h, 2))
+        pl.when(i == 2)(lambda: share_keys(1))
+        pl.when(i == 2)(lambda: take_keys(1))
+        for h in range(LOCAL_HEADS):
+            pl.when(i == 3)(functools.partial(ring_step, h, 3))
         for h in (0, 1):
-            pl.when(u == 0)(functools.partial(sum_step, h, 0))
-            pl.when(u == 2)(functools.partial(sum_step, h, 1))
-            pl.when(u == 5)(functools.partial(sum_step, h, 2))
+            pl.when(i == 6)(functools.partial(ring_end, h))
+        pl.when(i == 6)(lambda: share_keys(2))
+        pl.when(i == 7)(lambda: take_keys(2))
+        pl.when(i == 7)(lambda: ring_end(2))
+        even, odd, later = unit_at(2 * i), unit_at(2 * i + 1), unit_at(jnp.minimum(2 * i + 2, 23))
+        top = stage(even, scores0, top, odd, scores1)
+        add_own(*even)
+        send_y(*even)
+        top = stage(odd, scores1, top, later, scores0)
+        add_own(*odd)
+        send_y(*odd)
+
+        @pl.when(i >= 6)
+        def _():
+            lax.fori_loop(3 * i - 18, 3 * i - 15, join, 0)
+
+        pl.when(i == 11)(lambda: middle(0))
+
         return top
 
-    top = stage(None, None, None, (0, dest_at(0)), scores0)
-    lax.fori_loop(0, 8, first_heads, top)
-    take_keys(2)
-    ring_end(2)
-
-    def last_head(i, top):
-        even, odd, later = dest_at(2 * i), dest_at(2 * i + 1), dest_at(jnp.minimum(2 * i + 2, 7))
-        top = stage((2, even), scores0, top, (2, odd), scores1)
-        add_own(2, even)
-        pl.when(i == 0)(lambda: sum_step(2, 0))
-        top = stage((2, odd), scores1, top, (2, later), scores0)
-        add_own(2, odd)
-        for h in (0, 1):
-            pl.when(i == 0)(functools.partial(sum_step, h, 3))
-        return top
-
-    top = stage(None, None, None, (2, dest_at(0)), scores0)
-    lax.fori_loop(0, 4, last_head, top)
-    sum_step(2, 1)
-    sum_end(0)
-    sum_end(1)
-    sum_step(2, 2)
+    def join(p, carry):
+        join_y(*unit_at(p))
+        return carry
+
+    lax.fori_loop(0, 12, pair, stage(None, None, None, unit_at(0), scores0))
+    middle(1)
+    lax.fori_loop(18, 21, join, 0)
+    middle(2)
     finish(0)
+    lax.fori_loop(21, 24, join, 0)
     finish(1)
-    sum_step(2, 3)
-    sum_end(2)
     finish(2)
 
     drain(queries.at[0, pl.ds(0, 15 * ROWS), :], q_send)
@@ -422,16 +434,19 @@
         for side in (0, 1):
             for step in range(4):
                 ring_copy(h, step, side).wait_send()
-                for copy in sum_copies(h, step, side):
-                    copy.wait_send()
-        for copy in y_copies(h):
+        for k in range(8):
+            for copy in y_copies(h, (at.z + k) % 8):
+                copy.wait_send()
+        for slot in (0, 1, 2, 3, 6, 7):
+            for copy in z_copies(h, at.z, slot, 1):
+                copy.wait_send()
+        for copy in z_copies(h, at.z, 4 + at.z % 2, 1):
             copy.wait_send()
         drain(ready.at[pl.ds(0, 7 * ROWS), pl.ds(0, HEAD_DIM)], out_send.at[h])
         drain(out.at[0, :, pl.ds(0, MEMBERS * HEAD_DIM)], out_recv.at[h])
 
 
 def shards(q, sk, sv, ck, cv, block_list, list_len, tok_count, noise_levels, gate_table):
-    smem = pl.BlockSpec(memory_space=pltpu.SMEM)
     hbm = pl.BlockSpec(memory_space=pltpu.HBM)
     dma = pltpu.SemaphoreType.DMA
     bf, f32 = jnp.bfloat16, jnp.float32
@@ -439,9 +454,14 @@
     return pl.pallas_call(
         kernel,
         out_shape=jax.ShapeDtypeStruct((1, ROWS, MEMBERS * COLS), bf),
-        in_specs=[smem] * 4 + [hbm] * 6,
+        in_specs=[hbm] * 10,
         out_specs=hbm,
-        scratch_shapes=[pltpu.VMEM((CLEAN + 1, KEYS, HEAD_DIM), bf)] * 6
+        scratch_shapes=[
+            pltpu.SMEM((STRETCHES, LIST), jnp.int32),
+            *[pltpu.SMEM((STRETCHES,), jnp.int32)] * 3,
+            dma((4,)),
+        ]
+        + [pltpu.VMEM((CLEAN + 1, KEYS, HEAD_DIM), bf)] * 6
         + [
             pltpu.VMEM((heads, CLEAN + 1, KEYS, HEAD_DIM), bf),
             pltpu.VMEM((heads, CLEAN + 1, HEAD_DIM, KEYS), bf),
@@ -454,19 +474,17 @@
             pltpu.SMEM((STRETCHES, PER_SRC + 1), jnp.int32),
             pltpu.VMEM((heads, 8, HEAD_DIM, QUERIES), bf),
             pltpu.VMEM((heads, 8, 8, 128), f32),
-            pltpu.VMEM((heads, 3, 2, HEAD_DIM, QUERIES), bf),
-            pltpu.VMEM((heads, 3, 2, 8, 128), f32),
-            pltpu.VMEM((heads, 4, 2, HEAD_DIM, QUERIES), bf),
-            pltpu.VMEM((heads, 4, 2, 8, 128), f32),
-            pltpu.VMEM((heads, HEAD_DIM, 128), bf),
-            pltpu.VMEM((heads, 8, 128), f32),
-            pltpu.VMEM((heads, HEAD_DIM, 128), bf),
-            pltpu.VMEM((heads, 8, 128), f32),
+            pltpu.VMEM((heads, 8, HEAD_DIM, 128), bf),
+            pltpu.VMEM((heads, 8, 8, 128), f32),
+            pltpu.VMEM((heads, 8, HEAD_DIM, 128), bf),
+            pltpu.VMEM((heads, 8, 8, 128), f32),
+            pltpu.VMEM((heads, 8, HEAD_DIM, 128), bf),
+            pltpu.VMEM((heads, 8, 8, 128), f32),
             pltpu.VMEM((48, COLS), f32),
             pltpu.VMEM((128, COLS), bf),
             dma((heads, 2)), dma((heads, 2)), dma((heads, 2)), dma((heads, 2)), dma, dma,
-            dma((heads, 4, 2)), dma((heads, 4, 2)), dma((heads, 4, 2)), dma((heads, 4, 2)),
-            dma((heads, 4, 2)), dma((heads, 4, 2)), dma((heads, 2)), dma((heads, 2)), dma((heads,)), dma((heads,)), dma,
+            dma((heads, 4, 2)), dma((heads, 4, 2)), dma((heads, 8, 2)), dma((heads, 8, 2)),
+            dma((heads, 8, 2)), dma((heads, 8, 2)), dma((heads,)), dma((heads,)), dma,
         ],
         compiler_params=pltpu.CompilerParams(
             collective_id=0, has_side_effects=True, vmem_limit_bytes=58 * 1024 * 1024

time: 70.7 us -> 67.4 us (0.953)
  Pallas kernels: 69.1 us -> 65.1 us
    pallas_call x1, Pallas kernels: 69.1 us -> 65.1 us  [shards(): pl.pallas_call(kernel, out_shape=jax.ShapeDtypeStruct((1, ROWS, MEMBERS *...]
where the time goes in v1:
time: 67.4 us; the launch traced here: 66.7 us
  Pallas kernels  65.1 us (97%)
  local copies, waits for them, and re-layouts  1.54 us (2%)
    pallas_call x1, Pallas kernels, shards(): pl.pallas_call(kernel, out_shape=jax.ShapeDtypeStruct((1, ROWS, MEMBERS *...  65.1 us
    unnamed x1, local copies, waits for them, and re-layouts  1.54 us

profile of v1, /device:TPU:8, one launch (start us, length us, event | category | flops | bytes accessed | tf_op | source)
XLA Modules:
  0.0 66.7 jit_solution(13916820678149643783)
XLA Ops:
  0.0 65.1 %shard_map.100 = bf16[1,16,3072]{2,1,0:T(8,128)(2,1)} custom-call(s32[4,16]{1,0:T(4,128)} %block_list_hbm.1, s32[4]{0:T(128)} %list_len_hbm.1, s32[4]{0:T(128)} %tok_count_hbm.1, s32[4]{0:T(128)} %noise_levels_hbm.1, bf16[1,16,3072]{2,1,0:T(8,128)(2,1)} %q.1, bf16[1,16,3072]{2,1,0:T(8,128)(2,1)} %sk.1, bf16[1,16,3072]{2,1,0:T(8,128)(2,1)} %sv.1, ...), custom_call_target="tpu_custom_call" | custom-call | tf_op jit(solution)/shard_map/pallas_call | solution.py:454
  65.1 1.5 %copy.12 = bf16[1,16,3072]{2,1,0:T(8,128)(2,1)} copy(bf16[1,16,3072]{2,1,0:T(8,128)(2,1)} %shard_map.100) | data formatting | bytes 196608

commit v2 on v1

--- a/solution.py
+++ b/solution.py
@@ -23,32 +23,47 @@
 MASKED = -1e30
 UNUSED = 1e30
 SCALE = 1.4426950408889634 / math.sqrt(HEAD_DIM)
-AXES = ("zh", "x", "yh", "yl", "zl", "core")
-GROUP = [(dx, dl) for dx in (2, 1, 3, 0) for dl in (1, 0) if (dx, dl) != (0, 0)]
-PLANE = [(dx, dh, dl) for dx in (2, 1, 3, 0) for dh in (1, 0) for dl in (1, 0) if (dx, dh, dl) != (0, 0, 0)]
+AXES = ("zh", "xh", "xl", "yh", "yl", "zl", "core")
+WIDE = 2 * HEAD_DIM
+GROUP = [(0, 1), (1, 0), (3, 0), (2, 1), (1, 1), (3, 1), (2, 0)]
+PLANE = [(dx, dy) for dx in (2, 1, 3, 0) for dy in (2, 1, 3, 0) if (dx, dy) != (0, 0)]
 
 
 class Place:
     def __init__(self):
         for name in AXES:
             setattr(self, name, lax.axis_index(name))
-        self.z = self.zh * 2 + self.zl
-        self.member = self.x * 2 + self.yl
-
-    def peer(self, dx, dl):
-        px, pyl = (self.x + dx) % 4, (self.yl + dl) % 2
-        return {"x": px, "yl": pyl}, px * 2 + pyl
-
-    def in_plane(self, dx, dh, dl):
-        target, member = self.peer(dx, dl)
-        return dict(target, yh=(self.yh + dh) % 2), member
+        self.x, self.y, self.z = self.xh * 2 + self.xl, self.yh * 2 + self.yl, self.zh * 2 + self.zl
+        self.members = (self.x * 2 + self.yl, self.x * 2 + self.yl, self.y * 2 + self.xl)
+
+    def peer(self, h, d, dl):
+        if h < 2:
+            px, pyl = (self.x + d) % 4, (self.yl + dl) % 2
+            return {"xh": px // 2, "xl": px % 2, "yl": pyl}, px * 2 + pyl
+        py, pxl = (self.y + d) % 4, (self.xl + dl) % 2
+        return {"yh": py // 2, "yl": py % 2, "xl": pxl}, py * 2 + pxl
+
+    def in_plane(self, dx, dy):
+        px, py = (self.x + dx) % 4, (self.y + dy) % 4
+        target = {"xh": px // 2, "xl": px % 2, "yh": py // 2, "yl": py % 2}
+        return target, px * 2 + py % 2, py * 2 + px % 2
+
+    def half(self, h):
+        return jnp.where(h == 2, self.xh, self.yh)
+
+    def to_partner(self, h):
+        return {"xh": jnp.where(h == 2, 1 - self.xh, self.xh), "yh": jnp.where(h == 2, self.yh, 1 - self.yh)}
+
+    def position(self, h, index, core):
+        if h < 2:
+            space = ((index // 32) % 4) * 256 + self.yh * 128 + ((index // 16) % 2) * 64
+        else:
+            space = self.xh * 512 + ((index // 16) % 2) * 256 + ((index // 32) % 4) * 64
+        return space + self.zl * 32 + core * 16 + index % 16
 
     def to_z(self, step):
         other = (self.z + step + 8) % 8
         return {"zh": other // 2, "zl": other % 2}
-
-    def to_y(self):
-        return {"yh": 1 - self.yh}
 
     def to_core(self):
         return {"core": 1 - self.core}
@@ -69,6 +84,10 @@
 
 def drain(ref, sem):
     pltpu.make_async_copy(ref, ref, sem).wait()
+
+
+def head_columns(h, member):
+    return aligned(member * WIDE + h * HEAD_DIM if h < 2 else MEMBERS * WIDE + member * HEAD_DIM, HEAD_DIM)
 
 
 def aligned(start, size):
@@ -125,24 +144,31 @@
         copy.start()
     greet([at.in_plane(*off)[0] for off in PLANE] + [*[at.to_z(k) for k in (1, -1, 2, -2)], at.to_core()])
 
-    q_rows = aligned(at.yh * 128 + at.member * ROWS, ROWS)
-    q_dst = queries.at[at.z, q_rows, :]
+    q_dst = [
+        queries.at[at.z, aligned(at.yh * 128 + at.members[0] * ROWS, ROWS), pl.ds(0, WIDE)],
+        queries.at[at.z, aligned(at.xh * 128 + at.members[2] * ROWS, ROWS), pl.ds(WIDE, HEAD_DIM)],
+    ]
+
+    def q_src(member, other):
+        return [q.at[0, :, aligned(member * WIDE, WIDE)], q.at[0, :, head_columns(2, other)]]
+
     for off in PLANE:
-        target, member = at.in_plane(*off)
-        remote(q.at[0, :, aligned(member * COLS, COLS)], q_dst, q_send, q_recv, target).start()
-    pltpu.make_async_copy(q.at[0, :, aligned(at.member * COLS, COLS)], q_dst, q_recv).start()
-
-    slot = aligned((at.core * MEMBERS + at.member) * ROWS, ROWS)
+        target, member, other = at.in_plane(*off)
+        for src, dst in zip(q_src(member, other), q_dst):
+            remote(src, dst, q_send, q_recv, target).start()
+    for src, dst in zip(q_src(at.members[0], at.members[2]), q_dst):
+        pltpu.make_async_copy(src, dst, q_recv).start()
+
     my_half = aligned(at.core * 128, 128)
 
     def send_keys(h):
         for part, ref in enumerate((keys[h], values[h])):
-            dst = ref.at[:, slot, :]
+            dst = ref.at[:, aligned((at.core * MEMBERS + at.members[h]) * ROWS, ROWS), :]
             for off in GROUP:
-                target, member = at.peer(*off)
-                cols = aligned(member * COLS + h * HEAD_DIM, HEAD_DIM)
+                target, member = at.peer(h, *off)
+                cols = head_columns(h, member)
                 remote(staged.at[part, :, :, cols], dst, kv_send.at[h, part], kv_recv.at[h, part], target).start()
-            cols = aligned(at.member * COLS + h * HEAD_DIM, HEAD_DIM)
+            cols = head_columns(h, at.members[h])
             pltpu.make_async_copy(staged.at[part, :, :, cols], dst, kv_recv.at[h, part]).start()
 
     def share_copy(h, part):
@@ -183,14 +209,12 @@
         for side in (0, 1):
             ring_copy(h, 3, side).wait_recv()
 
-    my_lanes, other_lanes = aligned(at.yh * 128, 128), aligned((1 - at.yh) * 128, 128)
-
     def y_copies(h, dest):
+        target = at.to_partner(h)
+        src = sums.at[h, dest, :, aligned((1 - at.half(h)) * 128, 128)]
         return [
-            remote(
-                sums.at[h, dest, :, other_lanes], y_got.at[h, dest], y_send.at[h, dest, 0], y_recv.at[h, dest, 0], at.to_y()
-            ),
-            remote(stats.at[h, dest], y_got_stats.at[h, dest], y_send.at[h, dest, 1], y_recv.at[h, dest, 1], at.to_y()),
+            remote(src, y_got.at[h, dest], y_send.at[h, dest, 0], y_recv.at[h, dest, 0], target),
+            remote(stats.at[h, dest], y_got_stats.at[h, dest], y_send.at[h, dest, 1], y_recv.at[h, dest, 1], target),
         ]
 
     def send_y(h, dest):
@@ -236,17 +260,17 @@
 
             z_start(h, dest, 6 + side, (-2, 2)[side])
 
-    def pick_half(ref):
+    def pick_half(h, ref):
         tile = ref[...]
-        return [jnp.where(at.yh == 0, tile[i : i + 1], tile[i + 1 : i + 2]) for i in (0, 2)]
+        return [jnp.where(at.half(h) == 0, tile[i : i + 1], tile[i + 1 : i + 2]) for i in (0, 2)]
 
     def join_y(h, dest):
         for copy in y_copies(h, dest):
             copy.wait_recv()
         merged, top, total = merge(
             [
-                (sums[h, dest, :, my_lanes], *pick_half(stats.at[h, dest])),
-                (y_got[h, dest], *pick_half(y_got_stats.at[h, dest])),
+                (sums[h, dest, :, aligned(at.half(h) * 128, 128)], *pick_half(h, stats.at[h, dest])),
+                (y_got[h, dest], *pick_half(h, y_got_stats.at[h, dest])),
             ]
         )
         put_joined(h, dest, merged, top, total)
@@ -268,7 +292,7 @@
     def finish(h):
         parts = [own_part(h, at.z)] + [z_part(h, slot) for slot in (0, 1, 6, 7)]
         r = lax.broadcasted_iota(jnp.int32, (128, HEAD_DIM), 0)
-        position = (r // 32) * 256 + at.yh * 128 + ((r // 16) % 2) * 64 + at.zl * 32 + at.core * 16 + r % 16
+        position = at.position(h, r, at.core)
         keep = position < tok_count[stretch_out]
         cols = pl.ds(h * HEAD_DIM, HEAD_DIM)
         gate_row = gates[pl.ds(noise_levels[stretch_out], 1), :][:, h * HEAD_DIM : (h + 1) * HEAD_DIM]
@@ -278,11 +302,11 @@
         normed = (attended * lax.rsqrt(mean_sq + 1e-6)).T
         ready[:, cols] = jnp.where(keep, normed * gate_row, 0.0).astype(jnp.bfloat16)
 
-        dst = out.at[0, :, aligned(at.member * COLS + h * HEAD_DIM, HEAD_DIM)]
+        dst = out.at[0, :, head_columns(h, at.members[h])]
         for off in GROUP:
-            target, member = at.peer(*off)
+            target, member = at.peer(h, *off)
             remote(ready.at[aligned(member * ROWS, ROWS), cols], dst, out_send.at[h], out_recv.at[h], target).start()
-        pltpu.make_async_copy(ready.at[aligned(at.member * ROWS, ROWS), cols], dst, out_recv.at[h]).start()
+        pltpu.make_async_copy(ready.at[aligned(at.members[h] * ROWS, ROWS), cols], dst, out_recv.at[h]).start()
 
     def query_rows(h, dest):
         plane = (dest + 6) % 8
@@ -329,7 +353,7 @@
         @pl.when((dest + 6) % 8 // 2 == at.zh)
         def _():
             _, q_head = query_rows(h, dest)
-            bias = own_bias[...]
+            bias = own_bias[jnp.where(h == 2, 1, 0)]
             scores = dot_rows(kept[h, CLEAN], q_head) + jnp.concatenate([bias, bias], axis=1)
             shift = jnp.max(scores, axis=0, keepdims=True) * SCALE
             weights = jnp.exp2(scores * SCALE - shift)
@@ -344,13 +368,21 @@
                 sums[h, dest, :, lanes] = merged.astype(jnp.bfloat16)
                 write_stats(stats.at[h, dest], half, top, total_both)
 
-    gate_copy = pltpu.make_async_copy(gate_table.at[:, aligned(at.member * COLS, COLS)], gates, gate_sem)
+    gate_copies = [
+        pltpu.make_async_copy(
+            gate_table.at[:, aligned(at.members[0] * WIDE, WIDE)], gates.at[:, pl.ds(0, WIDE)], gate_sem.at[0]
+        ),
+        pltpu.make_async_copy(
+            gate_table.at[:, head_columns(2, at.members[2])], gates.at[:, pl.ds(WIDE, HEAD_DIM)], gate_sem.at[1]
+        ),
+    ]
 
     for copy in staging:
         copy.wait()
     for h in range(LOCAL_HEADS):
         send_keys(h)
-    gate_copy.start()
+    for copy in gate_copies:
+        copy.start()
     for copy in scalars:
         copy.wait()
     for stretch in range(STRETCHES):
@@ -366,15 +398,16 @@
             picked[stretch, e] = chosen[e]
         picked[stretch, PER_SRC] = count
     j = lax.broadcasted_iota(jnp.int32, (KEYS, 128), 0)
-    position = ((j // 32) % 4) * 256 + at.yh * 128 + ((j // 16) % 2) * 64 + at.zl * 32 + (j // 128) * 16 + j % 16
-    own_bias[...] = jnp.where(position < tok_count[at.zh], 0.0, MASKED)
+    for n, h in enumerate((0, 2)):
+        own_bias[n] = jnp.where(at.position(h, j % 128, j // 128) < tok_count[at.zh], 0.0, MASKED)
     drain(queries.at[at.z], q_recv)
-    for h in range(LOCAL_HEADS):
-        ring_step(h, 0)
-    for h in range(LOCAL_HEADS):
-        ring_step(h, 1)
+    for step in (0, 1):
+        for h in (0, 1):
+            ring_step(h, step)
+    ring_step(2, 0)
     share_keys(0)
-    gate_copy.wait()
+    for copy in gate_copies:
+        copy.wait()
     take_keys(0)
 
     def unit_at(p):
@@ -386,17 +419,20 @@
         return h, (at.z + jnp.where(far, near_first, far_first)) % 8
 
     def pair(i, top):
-        for h in range(LOCAL_HEADS):
+        for h in (0, 1):
             pl.when(i == 1)(functools.partial(ring_step, h, 2))
+        pl.when(i == 2)(lambda: ring_step(2, 1))
         pl.when(i == 2)(lambda: share_keys(1))
         pl.when(i == 2)(lambda: take_keys(1))
-        for h in range(LOCAL_HEADS):
+        for h in (0, 1):
             pl.when(i == 3)(functools.partial(ring_step, h, 3))
+        pl.when(i == 4)(lambda: ring_step(2, 2))
         for h in (0, 1):
             pl.when(i == 6)(functools.partial(ring_end, h))
+        pl.when(i == 6)(lambda: ring_step(2, 3))
         pl.when(i == 6)(lambda: share_keys(2))
         pl.when(i == 7)(lambda: take_keys(2))
-        pl.when(i == 7)(lambda: ring_end(2))
+        pl.when(i == 9)(lambda: ring_end(2))
         even, odd, later = unit_at(2 * i), unit_at(2 * i + 1), unit_at(jnp.minimum(2 * i + 2, 23))
         top = stage(even, scores0, top, odd, scores1)
         add_own(*even)
@@ -470,7 +506,7 @@
             pltpu.VMEM((2, CLEAN + 1, ROWS, MEMBERS * COLS), bf),
             dma((4,)),
             pltpu.VMEM((8, QUERIES, COLS), bf),
-            pltpu.VMEM((KEYS, 128), f32),
+            pltpu.VMEM((2, KEYS, 128), f32),
             pltpu.SMEM((STRETCHES, PER_SRC + 1), jnp.int32),
             pltpu.VMEM((heads, 8, HEAD_DIM, QUERIES), bf),
             pltpu.VMEM((heads, 8, 8, 128), f32),
@@ -484,7 +520,7 @@
             pltpu.VMEM((128, COLS), bf),
             dma((heads, 2)), dma((heads, 2)), dma((heads, 2)), dma((heads, 2)), dma, dma,
             dma((heads, 4, 2)), dma((heads, 4, 2)), dma((heads, 8, 2)), dma((heads, 8, 2)),
-            dma((heads, 8, 2)), dma((heads, 8, 2)), dma((heads,)), dma((heads,)), dma,
+            dma((heads, 8, 2)), dma((heads, 8, 2)), dma((heads,)), dma((heads,)), dma((2,)),
         ],
         compiler_params=pltpu.CompilerParams(
             collective_id=0, has_side_effects=True, vmem_limit_bytes=58 * 1024 * 1024
@@ -493,8 +529,8 @@
 
 
 def solution(mesh):
-    fine = Mesh(mesh.devices.reshape(4, 4, 2, 2, 2, 2), AXES)
-    split = P("zh", ("x", "yh", "yl", "zl", "core"), None)
+    fine = Mesh(mesh.devices.reshape(4, 2, 2, 2, 2, 2, 2), AXES)
+    split = P("zh", ("xh", "xl", "yh", "yl", "zl", "core"), None)
     return jax.shard_map(
         shards, mesh=fine, in_specs=(split,) * 5 + (P(),) * 5, out_specs=split, check_vma=False
     )

time: 67.4 us -> 66.8 us (level)
  no operation moved by 1% of the time
where the time goes in v2:
time: 66.8 us; the launch traced here: 66.5 us
  Pallas kernels  64.9 us (97%)
  local copies, waits for them, and re-layouts  1.54 us (2%)
    pallas_call x1, Pallas kernels, shards(): pl.pallas_call(kernel, out_shape=jax.ShapeDtypeStruct((1, ROWS, MEMBERS *...  64.9 us
    unnamed x1, local copies, waits for them, and re-layouts  1.54 us

profile of v2, /device:TPU:8, one launch (start us, length us, event | category | flops | bytes accessed | tf_op | source)
XLA Modules:
  0.0 66.5 jit_solution(10065034898975900662)
XLA Ops:
  0.0 64.9 %shard_map.100 = bf16[1,16,3072]{2,1,0:T(8,128)(2,1)} custom-call(s32[4,16]{1,0:T(4,128)} %block_list_hbm.1, s32[4]{0:T(128)} %list_len_hbm.1, s32[4]{0:T(128)} %tok_count_hbm.1, s32[4]{0:T(128)} %noise_levels_hbm.1, bf16[1,16,3072]{2,1,0:T(8,128)(2,1)} %q.1, bf16[1,16,3072]{2,1,0:T(8,128)(2,1)} %sk.1, bf16[1,16,3072]{2,1,0:T(8,128)(2,1)} %sv.1, ...), custom_call_target="tpu_custom_call" | custom-call | tf_op jit(solution)/shard_map/pallas_call | solution.py:490
  64.9 1.5 %copy.12 = bf16[1,16,3072]{2,1,0:T(8,128)(2,1)} copy(bf16[1,16,3072]{2,1,0:T(8,128)(2,1)} %shard_map.100) | data formatting | bytes 196608

commit v3 on v2

--- a/solution.py
+++ b/solution.py
@@ -355,8 +355,9 @@
             _, q_head = query_rows(h, dest)
             bias = own_bias[jnp.where(h == 2, 1, 0)]
             scores = dot_rows(kept[h, CLEAN], q_head) + jnp.concatenate([bias, bias], axis=1)
-            shift = jnp.max(scores, axis=0, keepdims=True) * SCALE
-            weights = jnp.exp2(scores * SCALE - shift)
+            top = jnp.max(scores, axis=0, keepdims=True)
+            shift = top * SCALE
+            weights = jnp.exp2(scores * SCALE - jnp.where(top > 0.5 * MASKED, shift, UNUSED))
             total = jnp.sum(weights, axis=0, keepdims=True)
             product = jnp.dot(turned[h, CLEAN], weights.astype(jnp.bfloat16), preferred_element_type=jnp.float32)
             before = read_stats(stats.at[h, dest])

time: 66.8 us -> 66.8 us (level)
  no operation moved by 1% of the time
where the time goes in v3:
time: 66.8 us; the launch traced here: 66.4 us
  Pallas kernels  64.9 us (97%)
  local copies, waits for them, and re-layouts  1.54 us (2%)
    pallas_call x1, Pallas kernels, shards(): pl.pallas_call(kernel, out_shape=jax.ShapeDtypeStruct((1, ROWS, MEMBERS *...  64.9 us
    unnamed x1, local copies, waits for them, and re-layouts  1.54 us

profile of v3, /device:TPU:8, one launch (start us, length us, event | category | flops | bytes accessed | tf_op | source)
XLA Modules:
  0.0 66.4 jit_solution(8420616996748597462)
XLA Ops:
  0.0 64.9 %shard_map.100 = bf16[1,16,3072]{2,1,0:T(8,128)(2,1)} custom-call(s32[4,16]{1,0:T(4,128)} %block_list_hbm.1, s32[4]{0:T(128)} %list_len_hbm.1, s32[4]{0:T(128)} %tok_count_hbm.1, s32[4]{0:T(128)} %noise_levels_hbm.1, bf16[1,16,3072]{2,1,0:T(8,128)(2,1)} %q.1, bf16[1,16,3072]{2,1,0:T(8,128)(2,1)} %sk.1, bf16[1,16,3072]{2,1,0:T(8,128)(2,1)} %sv.1, ...), custom_call_target="tpu_custom_call" | custom-call | tf_op jit(solution)/shard_map/pallas_call | solution.py:491
  64.9 1.5 %copy.12 = bf16[1,16,3072]{2,1,0:T(8,128)(2,1)} copy(bf16[1,16,3072]{2,1,0:T(8,128)(2,1)} %shard_map.100) | data formatting | bytes 196608
